TPU v7x, 32 devices: a whole 2x2x4 slice. The times are simulated.
32 devices in a mesh: groups: 2 (over y), ty: 4 (over z), tx: 2 (over x), pz: 2 (over core).
Axes of the slice: x: 2, y: 2, z: 4, core: 2. Of those that a mesh axis runs over, the one named last changes fastest.
Arguments:
- object_field: float32 [2, 2048, 512], P(None, ('groups', 'ty'), 'tx'), parts along dimension 1, may hold values from -6 to 6
- probe_wave: float32 [2, 256, 256], replicated, may hold values from -6 to 6
- amplitudes: float32 [192, 256, 256], P(('groups', 'ty', 'tx', 'pz')), parts along dimension 0, may hold values from 0.3 to 3
- positions: int32 [192, 2], P(('groups', 'ty', 'tx', 'pz')), parts along dimension 0, may hold values from 0 to 1023, as said below
- counts: int32 [32], P(('groups', 'ty', 'tx', 'pz')), parts along dimension 0, may hold values from 1 to 6, as said below
Outputs:
- object_grad: float32 [2, 2048, 512], P(None, ('groups', 'ty'), 'tx'), parts along dimension 1
- probe_grad: float32 [4, 256, 256], P('groups'), parts along dimension 0
There are 2 independent parts, one for each index of `groups`. A program takes and returns all parts, laid end to end along the dimension named above; an argument that names none is the same for every part. Nothing has to cross between parts.
Inputs may be any that keep to these rules, and one draw needn't show every extreme that they name: `positions`: the slots of owner d are rows d * 6 to d * 6 + 5. With owner d = (a * 2 + b) * 2 + c, every slot's row offset lies in a * 256 to a * 256 + 255 and its column offset in b * 256 to b * 256 + 255. `counts`: some owner uses all 6 slots in every draw.
All inputs are finite; a program needn't handle non-finite values.
Results may differ from a plain program's by a relative error of at most 0.0003.
Values sent between devices are 32-bit elements; how exact they have to be, the bound alone decides.
A program may use at most 64 MiB of HBM per device.

v0:
```python
import math

import jax
import jax.numpy as jnp
from jax import lax
from jax.sharding import PartitionSpec as P


def passed_along(value, axis, by):
    peers = lax.axis_size(axis)
    return lax.ppermute(value, axis, [(i, (i + by) % peers) for i in range(peers)])


def dft_tables(probe_size):
    ladder = jnp.arange(probe_size, dtype=jnp.int32)
    product = ladder[:, None] * ladder[None, :] % probe_size
    phase = product.astype(jnp.float32) * (2.0 * math.pi / probe_size)
    factor = 1.0 / math.sqrt(probe_size)
    return (jnp.cos(phase) * factor, -jnp.sin(phase) * factor)


def matmul(left, right):
    return jnp.dot(left, right, precision=lax.Precision.HIGHEST, preferred_element_type=jnp.float32)


def transform(real_part, imag_part, cos_tab, sin_tab):
    mid_re = matmul(cos_tab, real_part) - matmul(sin_tab, imag_part)
    mid_im = matmul(cos_tab, imag_part) + matmul(sin_tab, real_part)
    out_re = matmul(mid_re, cos_tab) - matmul(mid_im, sin_tab)
    out_im = matmul(mid_re, sin_tab) + matmul(mid_im, cos_tab)
    return (out_re, out_im)


def slot_grad(patch_view, probe_wave, amplitude, valid_mask, cos_tab, sin_tab):
    probe_re, probe_im = (probe_wave[0], probe_wave[1])
    patch_re, patch_im = (patch_view[0], patch_view[1])
    exit_re = probe_re * patch_re - probe_im * patch_im
    exit_im = probe_re * patch_im + probe_im * patch_re
    far_re, far_im = transform(exit_re, exit_im, cos_tab, sin_tab)
    magnitude = jnp.sqrt(far_re * far_re + far_im * far_im + 0.01)
    resid_re = valid_mask * (far_re - amplitude * far_re / magnitude)
    resid_im = valid_mask * (far_im - amplitude * far_im / magnitude)
    back_re, back_im = transform(resid_re, resid_im, cos_tab, -sin_tab)
    patch_grad = jnp.stack(
        [probe_re * back_re + probe_im * back_im, probe_re * back_im - probe_im * back_re]
    )
    probe_term = jnp.stack(
        [patch_re * back_re + patch_im * back_im, patch_re * back_im - patch_im * back_re]
    )
    return (patch_grad, probe_term)


def per_device(object_field, probe_wave, amplitudes, positions, counts):
    probe_size = probe_wave.shape[1]
    tile_h = object_field.shape[1]
    tile_w = object_field.shape[2]
    slot_count = positions.shape[0]
    cos_tab, sin_tab = dft_tables(probe_size)
    right_tile = passed_along(object_field, "tx", -1)
    upper_band = jnp.concatenate([object_field, right_tile], axis=2)
    lower_band = passed_along(upper_band, "ty", -1)
    extended = jnp.concatenate([upper_band, lower_band], axis=1)
    row_base = lax.axis_index("ty") * tile_h
    col_base = lax.axis_index("tx") * tile_w
    zero_index = jnp.zeros((), jnp.int32)
    used_count = counts[0]

    def visit_slot(slot_index, loop_state):
        grad_buffer, probe_acc = loop_state
        position = lax.dynamic_index_in_dim(positions, slot_index, 0, keepdims=False)
        amplitude = lax.dynamic_index_in_dim(amplitudes, slot_index, 0, keepdims=False)
        corner = (zero_index, position[0] - row_base, position[1] - col_base)
        patch_view = lax.dynamic_slice(extended, corner, (2, probe_size, probe_size))
        valid_mask = (slot_index < used_count).astype(jnp.float32)
        patch_grad, probe_term = slot_grad(
            patch_view, probe_wave, amplitude, valid_mask, cos_tab, sin_tab
        )
        current = lax.dynamic_slice(grad_buffer, corner, (2, probe_size, probe_size))
        grad_buffer = lax.dynamic_update_slice(grad_buffer, current + patch_grad, corner)
        return (grad_buffer, probe_acc + probe_term)

    start_buffer = jnp.zeros((2, 2 * tile_h, 2 * tile_w), jnp.float32)
    start_probe = jnp.zeros((2, probe_size, probe_size), jnp.float32)
    grad_buffer, probe_acc = lax.fori_loop(0, slot_count, visit_slot, (start_buffer, start_probe))
    received = passed_along(grad_buffer[:, :, tile_w:], "tx", 1)
    column_strip = grad_buffer[:, :, :tile_w] + received
    received_down = passed_along(column_strip[:, tile_h:, :], "ty", 1)
    tile_part = column_strip[:, :tile_h, :] + received_down
    object_grad = lax.psum(tile_part, "pz")
    probe_grad = lax.psum(probe_acc, ("ty", "tx", "pz"))
    return (object_grad, probe_grad)


def solution(mesh):
    return jax.shard_map(
        per_device,
        mesh=mesh,
        in_specs=(
            P(None, ("groups", "ty"), "tx"),
            P(),
            P(("groups", "ty", "tx", "pz"), None, None),
            P(("groups", "ty", "tx", "pz"), None),
            P(("groups", "ty", "tx", "pz")),
        ),
        out_specs=(P(None, ("groups", "ty"), "tx"), P("groups", None, None)),
        check_vma=False,
    )
```

profile of v0, /device:TPU:0, one launch (start us, length us, event | category | flops | bytes accessed | tf_op | source)
XLA Modules:
  0.0 421.2 jit_solution(8480106104176563090)
XLA Ops:
  7.2 3.0 collective-permute-start
  11.4 11.0 %collective-permute-done = f32[2,256,256]{2,1,0:T(8,128)S(1)} collective-permute-done((f32[2,256,256]{2,1,0:T(8,128)}, f32[2,256,256]{2,1,0:T(8,128)S(1)}, u32[]{:S(2)}, u32[]{:S(2)}) %collective-permute-start) | collective-permute-done | bytes 524320 | tf_op jit(solution)/shard_map/ppermute | solution.py:11
  22.4 3.9 collective-permute-start.1
  26.3 21.5 %collective-permute-done.1 = f32[2,256,512]{2,1,0:T(8,128)} collective-permute-done((f32[2,256,512]{2,1,0:T(8,128)S(1)}, f32[2,256,512]{2,1,0:T(8,128)}, u32[]{:S(2)}, u32[]{:S(2)}) %collective-permute-start.1) | collective-permute-done | bytes 1048608 | tf_op jit(solution)/shard_map/ppermute | solution.py:11
  47.9 1.7 pad_maximum_fusion
  49.6 1.6 broadcast_in_dim.8
  51.2 217.6 %while.18 = (s32[]{:T(128)}, f32[2,512,512]{2,1,0:T(8,128)}, f32[2,256,256]{2,1,0:T(8,128)}, s32[6,2]{0,1:T(2,128)S(1)}, s32[]{:T(128)}, /*index=5*/s32[]{:T(128...) while((s32[]{:T(128)}, f32[2,512,512]{2,1,0:T(8,128)}, ...), condition=%wide.region_1.2_spmd.clone.clone, body=%wide.region_0.1_spmd.clone.clone.sunk | while | flops 3240886272 | bytes 23331220 | solution.py:84
  64.4 2.6 fusion.192
  77.3 1.6 add_bitcast_fusion.2
  81.2 5.9 %dynamic_update_slice.11 = f32[2,512,512]{2,1,0:T(8,128)} dynamic-update-slice(f32[2,512,512]{2,1,0:T(8,128)} %get-tuple-element.515, f32[2,256,256]{2,1,0:T(8,128)S(1)} %get-tuple-element.498, s32[]{:T(128)} %constant.71.clone.1..sunk, s32[]{:T(128)S(6)} %select_n.154, s32[]{:T(128)S(6)} %select_n.155) | dynamic-update-slice | bytes 1048580 | tf_op jit(solution)/shard_map/while/body/eval_jaxpr/dynamic_update_slice | solution.py:79
  100.3 2.6 fusion.192
  113.2 1.6 add_bitcast_fusion.2
  117.1 6.0 %dynamic_update_slice.11 = f32[2,512,512]{2,1,0:T(8,128)} dynamic-update-slice(f32[2,512,512]{2,1,0:T(8,128)} %get-tuple-element.515, f32[2,256,256]{2,1,0:T(8,128)S(1)} %get-tuple-element.498, s32[]{:T(128)} %constant.71.clone.1..sunk, s32[]{:T(128)S(6)} %select_n.154, s32[]{:T(128)S(6)} %select_n.155) | dynamic-update-slice | bytes 1048580 | tf_op jit(solution)/shard_map/while/body/eval_jaxpr/dynamic_update_slice | solution.py:79
  136.3 2.6 fusion.192
  149.2 1.6 add_bitcast_fusion.2
  153.1 6.2 %dynamic_update_slice.11 = f32[2,512,512]{2,1,0:T(8,128)} dynamic-update-slice(f32[2,512,512]{2,1,0:T(8,128)} %get-tuple-element.515, f32[2,256,256]{2,1,0:T(8,128)S(1)} %get-tuple-element.498, s32[]{:T(128)} %constant.71.clone.1..sunk, s32[]{:T(128)S(6)} %select_n.154, s32[]{:T(128)S(6)} %select_n.155) | dynamic-update-slice | bytes 1048580 | tf_op jit(solution)/shard_map/while/body/eval_jaxpr/dynamic_update_slice | solution.py:79
  172.6 2.6 fusion.192
  185.5 1.6 add_bitcast_fusion.2
  189.4 6.4 %dynamic_update_slice.11 = f32[2,512,512]{2,1,0:T(8,128)} dynamic-update-slice(f32[2,512,512]{2,1,0:T(8,128)} %get-tuple-element.515, f32[2,256,256]{2,1,0:T(8,128)S(1)} %get-tuple-element.498, s32[]{:T(128)} %constant.71.clone.1..sunk, s32[]{:T(128)S(6)} %select_n.154, s32[]{:T(128)S(6)} %select_n.155) | dynamic-update-slice | bytes 1048580 | tf_op jit(solution)/shard_map/while/body/eval_jaxpr/dynamic_update_slice | solution.py:79
  209.0 2.6 fusion.192
  221.9 1.6 add_bitcast_fusion.2
  225.8 6.5 %dynamic_update_slice.11 = f32[2,512,512]{2,1,0:T(8,128)} dynamic-update-slice(f32[2,512,512]{2,1,0:T(8,128)} %get-tuple-element.515, f32[2,256,256]{2,1,0:T(8,128)S(1)} %get-tuple-element.498, s32[]{:T(128)} %constant.71.clone.1..sunk, s32[]{:T(128)S(6)} %select_n.154, s32[]{:T(128)S(6)} %select_n.155) | dynamic-update-slice | bytes 1048580 | tf_op jit(solution)/shard_map/while/body/eval_jaxpr/dynamic_update_slice | solution.py:79
  245.4 2.6 fusion.192
  262.3 6.6 %dynamic_update_slice.11 = f32[2,512,512]{2,1,0:T(8,128)} dynamic-update-slice(f32[2,512,512]{2,1,0:T(8,128)} %get-tuple-element.515, f32[2,256,256]{2,1,0:T(8,128)S(1)} %get-tuple-element.498, s32[]{:T(128)} %constant.71.clone.1..sunk, s32[]{:T(128)S(6)} %select_n.154, s32[]{:T(128)S(6)} %select_n.155) | dynamic-update-slice | bytes 1048580 | tf_op jit(solution)/shard_map/while/body/eval_jaxpr/dynamic_update_slice | solution.py:79
  270.3 2.7 collective-permute-start.2
  273.0 21.5 %collective-permute-done.2 = f32[2,512,256]{2,1,0:T(8,128)S(1)} collective-permute-done((f32[2,512,256]{2,1,0:T(8,128)S(1)}, f32[2,512,256]{2,1,0:T(8,128)S(1)}, u32[]{:S(2)}, u32[]{:S(2)}) %collective-permute-start.2) | collective-permute-done | bytes 1048608 | tf_op jit(solution)/shard_map/ppermute | solution.py:11
  296.2 14.9 %collective-permute-done.3 = f32[2,256,256]{2,1,0:T(8,128)S(1)} collective-permute-done((f32[2,256,256]{2,1,0:T(8,128)S(1)}, f32[2,256,256]{2,1,0:T(8,128)S(1)}, u32[]{:S(2)}, u32[]{:S(2)}) %collective-permute-start.3) | collective-permute-done | bytes 524320 | tf_op jit(solution)/shard_map/ppermute | solution.py:11
  311.0 1.9 slice_add_fusion.1
  313.0 75.5 %all-reduce.5.cloned.1.call-done = f32[2,256,256]{2,1,0:T(8,128)} async-done(((f32[2,256,256]{2,1,0:T(8,128)}), f32[2,256,256]{2,1,0:T(8,128)}) %all-reduce.5.cloned.1.call-update) | async-done | bytes 524304 | tf_op jit(solution)/shard_map/psum | solution.py:90
  388.5 22.2 %all-reduce.3.cloned.1.call-done = f32[2,256,256]{2,1,0:T(8,128)} async-done(((f32[2,256,256]{2,1,0:T(8,128)}), f32[2,256,256]{2,1,0:T(8,128)}) %all-reduce.3.cloned.1.call-update) | async-done | bytes 524304 | tf_op jit(solution)/shard_map/psum | solution.py:89
  410.7 1.9 copy.20
  412.5 1.9 copy.21
  (154 shorter events, 148.7 us)
Async XLA Ops:
  7.2 381.3 %all-reduce.5.cloned.1.call-start = ((), (), s32[]{:S(2)}) async-start(), calls=%async_computation.1 | async-start | bytes 1048576 | tf_op jit(solution)/shard_map/psum | solution.py:90
  7.2 15.1 %collective-permute-start = (f32[2,256,256]{2,1,0:T(8,128)}, f32[2,256,256]{2,1,0:T(8,128)S(1)}, u32[]{:S(2)}, u32[]{:S(2)}) collective-permute-start(f32[2,256,256]{2,1,0:T(8,128)} %param.7), channel_id=1, source_target_pairs={{0,2},{2,0},{1,3},{3,1},{4,6},{6,4},{5,7},{7,5},{8,10},{10,8},{9,1... | collective-permute-start | bytes 1572872 | tf_op jit(solution)/shard_map/ppermute | solution.py:11
  22.4 3.9 copy-start.5
  22.4 25.4 %collective-permute-start.1 = (f32[2,256,512]{2,1,0:T(8,128)S(1)}, f32[2,256,512]{2,1,0:T(8,128)}, u32[]{:S(2)}, u32[]{:S(2)}) collective-permute-start(f32[2,256,512]{2,1,0:T(8,128)S(1)} %constant_dynamic-update-slice_fusion), channel_id=1, source_target_pairs={{0,12},{4,0},{8,4},{12,8},{1,13},{5,1},{9,5},{13,9},{2,14},{6,2},{... | collective-permute-start | bytes 3145736 | tf_op jit(solution)/shard_map/ppermute | solution.py:11
  49.6 1.6 copy-start
  49.6 1.6 copy-start.6
  75.8 3.1 copy-start.2
  80.4 0.8 copy-start.3
  111.7 3.1 copy-start.2
  116.3 0.8 copy-start.3
  147.8 3.1 copy-start.2
  152.3 0.8 copy-start.3
  184.0 3.1 copy-start.2
  188.6 0.8 copy-start.3
  220.4 3.1 copy-start.2
  225.0 0.8 copy-start.3
  256.9 3.1 copy-start.2
  261.5 0.8 copy-start.3
  268.8 25.6 %copy-start.1 = (f32[2,512,512]{2,1,0:T(8,128)S(1)}, f32[2,512,512]{2,1,0:T(8,128)}, u32[]{:S(2)}) copy-start(f32[2,512,512]{2,1,0:T(8,128)} %get-tuple-element.294) | copy-start | bytes 6291460
  270.3 24.2 %collective-permute-start.2 = (f32[2,512,256]{2,1,0:T(8,128)S(1)}, f32[2,512,256]{2,1,0:T(8,128)S(1)}, u32[]{:S(2)}, u32[]{:S(2)}) collective-permute-start(f32[2,512,256]{2,1,0:T(8,128)S(1)} %slice.63), channel_id=1, source_target_pairs={{0,2},{2,0},{1,3},{3,1},{4,6},{6,4},{5,7},{7,5},{8,10},{10,8},{9,1... | collective-permute-start | bytes 3145736 | tf_op jit(solution)/shard_map/ppermute | solution.py:11
  294.7 1.0 copy-start.4
  295.7 15.3 %collective-permute-start.3 = (f32[2,256,256]{2,1,0:T(8,128)S(1)}, f32[2,256,256]{2,1,0:T(8,128)S(1)}, u32[]{:S(2)}, u32[]{:S(2)}) collective-permute-start(f32[2,256,256]{2,1,0:T(8,128)S(1)} %slice.79), channel_id=1, source_target_pairs={{0,4},{4,8},{8,12},{12,0},{1,5},{5,9},{9,13},{13,1},{2,6},{6,10},{... | collective-permute-start | bytes 1572872 | tf_op jit(solution)/shard_map/ppermute | solution.py:11
  296.1 114.5 %all-reduce.3.cloned.1.call-start = ((), (), s32[]{:S(2)}) async-start(), calls=%async_computation | async-start | bytes 1048576 | tf_op jit(solution)/shard_map/psum | solution.py:89
Sparse Core Ops, SparseCore 0:
  296.3 92.1 all-reduce.4
  391.4 19.2 all-reduce.2
where the time goes:
time: 423 us; the launch traced here: 421 us
  waiting for transfers between devices  167 us (39%)
  matrix products  148 us (35%)
  local copies, waits for them, and re-layouts  55.4 us (13%)
  other arithmetic  14.1 us (3%)
  between operations  14.1 us (3%)
  loops' own time  12.4 us (3%)
  starting transfers between devices  10.1 us (2%)
    dot_general x96, matrix products, matmul(): jnp.dot(left, right, precision=lax.Precision.HIGHEST, preferred_element_t...  148 us
    psum x1, waiting for transfers between devices, per_device(): probe_grad = lax.psum(probe_acc, ('ty', 'tx', 'pz'))  75.5 us
    ppermute x4, waiting for transfers between devices, passed_along(): lax.ppermute(value, axis, [(i, (i + by) % peers) for i in range(peers)])  68.9 us
    dynamic_update_slice x6, local copies, waits for them, and re-layouts, visit_slot(): lax.dynamic_update_slice(grad_buffer, current + patch_grad, corner)  37.6 us
    psum x1, waiting for transfers between devices, per_device(): object_grad = lax.psum(tile_part, 'pz')  22.2 us
    another operation x1, loops' own time, per_device(): lax.fori_loop(0, slot_count, visit_slot, (start_buffer, start_probe))  12.4 us
    ppermute x4, starting transfers between devices, passed_along(): lax.ppermute(value, axis, [(i, (i + by) % peers) for i in range(peers)])  10 us
    add x6, other arithmetic, visit_slot(): current + patch_grad  8.94 us
  transfers between devices with their start and end apart: 6, of which 6 were waited for; matrix products, arithmetic and copies ran while one was open for 1% of the time, Pallas kernels for 0%

commit v1 on v0

v1 whole, which is shorter than its diff:
```python
import functools

import jax
import jax.numpy as jnp
import numpy as np
from jax import lax
from jax.experimental import pallas as pl
from jax.experimental.pallas import tpu as pltpu
from jax.sharding import PartitionSpec as P


def passed_along(value, axis, by):
    peers = lax.axis_size(axis)
    return lax.ppermute(value, axis, [(i, (i + by) % peers) for i in range(peers)])


def half_tables(size):
    half = size // 2
    pixel = np.arange(half)
    tables = []
    for parity in (0, 1):
        freq = 2 * np.arange(half) + parity
        phase = (freq[:, None] * pixel[None, :] % size) * (2.0 * np.pi / size)
        cos_tab = np.cos(phase) / np.sqrt(size)
        sin_tab = np.sin(phase) / np.sqrt(size)
        full = np.block([[cos_tab, sin_tab], [-sin_tab, cos_tab]])
        tables += [full, full.T]
    full = np.stack(tables)
    high = full.astype(jnp.bfloat16)
    low = (full - high.astype(np.float64)).astype(jnp.bfloat16)
    return np.stack([high, low], axis=1)


def order_table(size):
    order = np.concatenate([np.arange(0, size, 2), np.arange(1, size, 2)])
    table = np.zeros((size, size), np.float32)
    table[order, np.arange(size)] = 1.0
    return table.astype(jnp.bfloat16)


def split(value):
    high = value.astype(jnp.bfloat16)
    low = (value - high.astype(jnp.float32)).astype(jnp.bfloat16)
    return high, low


def mm(left, right):
    return jnp.dot(left, right, preferred_element_type=jnp.float32)


def left_product(tab_ref, which, value):
    high, low = split(value)
    return mm(tab_ref[which, 0], high) + mm(tab_ref[which, 0], low) + mm(tab_ref[which, 1], high)


def right_product(tab_ref, which, value):
    high, low = split(value)
    return mm(high, tab_ref[which, 0]) + mm(low, tab_ref[which, 0]) + mm(high, tab_ref[which, 1])


def forward(re, im, tab_ref):
    half = re.shape[0] // 2
    cat = jnp.concatenate
    even = cat([re[:half] + re[half:], im[:half] + im[half:]], 0)
    odd = cat([re[:half] - re[half:], im[:half] - im[half:]], 0)
    even = left_product(tab_ref, 0, even)
    odd = left_product(tab_ref, 2, odd)
    re = cat([even[:half], odd[:half]], 0)
    im = cat([even[half:], odd[half:]], 0)
    even = cat([re[:, :half] + re[:, half:], im[:, :half] + im[:, half:]], 1)
    odd = cat([re[:, :half] - re[:, half:], im[:, :half] - im[:, half:]], 1)
    even = right_product(tab_ref, 1, even)
    odd = right_product(tab_ref, 3, odd)
    return cat([even[:, :half], odd[:, :half]], 1), cat([even[:, half:], odd[:, half:]], 1)


def backward(re, im, tab_ref):
    half = re.shape[0] // 2
    cat = jnp.concatenate
    even = right_product(tab_ref, 0, cat([re[:, :half], im[:, :half]], 1))
    odd = right_product(tab_ref, 2, cat([re[:, half:], im[:, half:]], 1))
    total, diff = even + odd, even - odd
    re = cat([total[:, :half], diff[:, :half]], 1)
    im = cat([total[:, half:], diff[:, half:]], 1)
    even = left_product(tab_ref, 1, cat([re[:half], im[:half]], 0))
    odd = left_product(tab_ref, 3, cat([re[half:], im[half:]], 0))
    total, diff = even + odd, even - odd
    return cat([total[:half], diff[:half]], 0), cat([total[half:], diff[half:]], 0)


def rolled(value, rows, cols):
    return pltpu.roll(pltpu.roll(value, rows, 0), cols, 1)


def compute_kernel(
    pos_ref, cnt_ref, own_ref, right_ref, down_ref, diag_ref, probe_ref, amp_ref, tab_ref, ord_ref,
    grad_ref, pgrad_ref, held_ref, ampl_ref, sem_ref,
):
    slots, size = amp_ref.shape[0], amp_ref.shape[1]
    amp_copies = [
        pltpu.make_async_copy(
            amp_ref.at[:, :, pl.ds(part * 128, 128)], ampl_ref.at[part], sem_ref.at[part]
        )
        for part in range(size // 128)
    ]
    for copy in amp_copies:
        copy.start()
    row_base = lax.axis_index("ty") * size
    col_base = lax.axis_index("tx") * size
    used_count = cnt_ref[0]
    half = size // 2
    row_id = lax.broadcasted_iota(jnp.int32, (size, size), 0)
    col_id = lax.broadcasted_iota(jnp.int32, (size, size), 1)
    pgrad_ref[...] = jnp.zeros_like(pgrad_ref)
    for copy in amp_copies:
        copy.wait()

    def visit(slot, carry):
        row = pos_ref[slot, 0] - row_base
        col = pos_ref[slot, 1] - col_base
        used = (slot < used_count).astype(jnp.float32)
        above = row_id < row
        before = col_id < col
        patch = [
            jnp.where(
                above,
                jnp.where(before, diag_ref[p], down_ref[p]),
                jnp.where(before, right_ref[p], own_ref[p]),
            )
            for p in range(2)
        ]
        probe = [rolled(probe_ref[p], row, col) for p in range(2)]
        exit_re = probe[0] * patch[0] - probe[1] * patch[1]
        exit_im = probe[0] * patch[1] + probe[1] * patch[0]
        far_re, far_im = forward(exit_re, exit_im, tab_ref)
        amp = jnp.concatenate(
            [
                jnp.concatenate(
                    [ampl_ref[part, slot, pl.ds(parity, half, 2), :] for part in range(size // 128)], 1
                )
                for parity in (0, 1)
            ],
            0,
        )
        high, low = split(amp)
        amp = mm(high, ord_ref[...]) + mm(low, ord_ref[...])
        gain = used * (1.0 - amp * lax.rsqrt(far_re * far_re + far_im * far_im + 0.01))
        back_re, back_im = backward(far_re * gain, far_im * gain, tab_ref)
        held_ref[slot, 0] = probe[0] * back_re + probe[1] * back_im
        held_ref[slot, 1] = probe[0] * back_im - probe[1] * back_re
        up, left = (size - row) % size, (size - col) % size
        pgrad_ref[0] += rolled(patch[0] * back_re + patch[1] * back_im, up, left)
        pgrad_ref[1] += rolled(patch[0] * back_im - patch[1] * back_re, up, left)
        return carry

    lax.fori_loop(0, slots, visit, 0)

    chunk = 16

    def gather(step, carry):
        base = pl.multiple_of(step * chunk, chunk)
        row_part = base + lax.broadcasted_iota(jnp.int32, (chunk, size), 0)
        col_part = lax.broadcasted_iota(jnp.int32, (chunk, size), 1)
        for p in range(2):
            sums = [jnp.zeros((chunk, size), jnp.float32) for _ in range(4)]
            for slot in range(slots):
                above = row_part < pos_ref[slot, 0] - row_base
                before = col_part < pos_ref[slot, 1] - col_base
                part = held_ref[slot, p, pl.ds(base, chunk), :]
                low = jnp.where(above, part, 0.0)
                top = part - low
                low_left = jnp.where(before, low, 0.0)
                top_left = jnp.where(before, top, 0.0)
                sums = [
                    sums[0] + (top - top_left),
                    sums[1] + top_left,
                    sums[2] + (low - low_left),
                    sums[3] + low_left,
                ]
            for quad in range(4):
                grad_ref[quad, p, pl.ds(base, chunk), :] = sums[quad]
        return carry

    lax.fori_loop(0, size // chunk, gather, 0)


def per_device(object_field, probe_wave, amplitudes, positions, counts):
    size = probe_wave.shape[1]
    slots = positions.shape[0]
    right = passed_along(object_field, "tx", -1)
    down = passed_along(object_field, "ty", -1)
    diag = passed_along(right, "ty", -1)
    vmem = pl.BlockSpec(memory_space=pltpu.VMEM)
    smem = pl.BlockSpec(memory_space=pltpu.SMEM)
    grads, probe_part = pl.pallas_call(
        compute_kernel,
        out_shape=(
            jax.ShapeDtypeStruct((4, 2, size, size), jnp.float32),
            jax.ShapeDtypeStruct((2, size, size), jnp.float32),
        ),
        in_specs=[smem, smem] + [vmem] * 5 + [pl.BlockSpec(memory_space=pl.ANY)] + [vmem] * 2,
        out_specs=(vmem, vmem),
        scratch_shapes=[
            pltpu.VMEM((slots, 2, size, size), jnp.float32),
            pltpu.VMEM((size // 128, slots, size, 128), jnp.float32),
            pltpu.SemaphoreType.DMA((size // 128,)),
        ],
        compiler_params=pltpu.CompilerParams(vmem_limit_bytes=48 * 1024 * 1024),
    )(
        positions, counts, object_field, right, down, diag, probe_wave, amplitudes,
        jnp.asarray(half_tables(size)), jnp.asarray(order_table(size)),
    )
    probe_grad = lax.psum(probe_part, ("ty", "tx", "pz"))
    from_right = passed_along(jnp.stack([grads[1], grads[3]]), "tx", 1)
    from_down = passed_along(grads[2] + from_right[1], "ty", 1)
    object_grad = lax.psum(grads[0] + from_right[0] + from_down, "pz")
    return object_grad, probe_grad


def solution(mesh):
    return jax.shard_map(
        per_device,
        mesh=mesh,
        in_specs=(
            P(None, ("groups", "ty"), "tx"),
            P(),
            P(("groups", "ty", "tx", "pz"), None, None),
            P(("groups", "ty", "tx", "pz"), None),
            P(("groups", "ty", "tx", "pz")),
        ),
        out_specs=(P(None, ("groups", "ty"), "tx"), P("groups", None, None)),
        check_vma=False,
    )
```

time: 423 us -> 211 us (0.50)
  matrix products: 148 us -> 0 us
  local copies, waits for them, and re-layouts: 55.4 us -> 11.6 us
  Pallas kernels: 0 us -> 16.7 us
  waiting for transfers between devices: 167 us -> 152 us
  loops' own time: 12.4 us -> 0 us
  other arithmetic: 14.1 us -> 2.88 us
    dot_general x96 -> x0, matrix products: 148 us -> none  [matmul(): jnp.dot(left, right, precision=lax.Precision.HIGHEST, preferred_element_t...]
    dynamic_update_slice x6 -> x0, local copies, waits for them, and re-layouts: 37.6 us -> none  [visit_slot(): lax.dynamic_update_slice(grad_buffer, current + patch_grad, corner)]
    pallas_call x0 -> x1, Pallas kernels: none -> 16.7 us  [per_device(): pl.pallas_call(compute_kernel, out_shape=(jax.ShapeDtypeStruct((4, 2, siz...]
    ppermute x4 -> x5, waiting for transfers between devices: 68.9 us -> 52.9 us  [passed_along(): lax.ppermute(value, axis, [(i, (i + by) % peers) for i in range(peers)])]
    another operation x1 -> x0, loops' own time: 12.4 us -> none  [per_device(): lax.fori_loop(0, slot_count, visit_slot, (start_buffer, start_probe))]
    add x14 -> x2, other arithmetic: 12.3 us -> 2.79 us  [the longest x1 1.93 us: per_device(): object_grad = lax.psum(grads[0] + from_right[0] + from_down, 'pz')]
    while x24 -> x0, local copies, waits for them, and re-layouts: 4.77 us -> none
    unnamed x13 -> x15, local copies, waits for them, and re-layouts: 5.87 us -> 10.1 us
  transfers between devices with their start and end apart: 6 -> 7, of which waited for: 6 -> 6; matrix products, arithmetic and copies ran while one was open for 1% -> 1% of each run, Pallas kernels for 0% -> 0%
where the time goes in v1:
time: 211 us
  waiting for transfers between devices  152 us (72%)
  Pallas kernels  16.7 us (8%)
  between operations  14.7 us (7%)
  starting transfers between devices  12.5 us (6%)
  local copies, waits for them, and re-layouts  11.6 us (5%)
  other arithmetic  2.88 us (1%)
    psum x1, waiting for transfers between devices, per_device(): probe_grad = lax.psum(probe_part, ('ty', 'tx', 'pz'))  77.2 us
    ppermute x5, waiting for transfers between devices, passed_along(): lax.ppermute(value, axis, [(i, (i + by) % peers) for i in range(peers)])  52.9 us
    psum x1, waiting for transfers between devices, per_device(): object_grad = lax.psum(grads[0] + from_right[0] + from_down, 'pz')  22.2 us
    pallas_call x1, Pallas kernels, per_device(): pl.pallas_call(compute_kernel, out_shape=(jax.ShapeDtypeStruct((4, 2, siz...  16.7 us
    ppermute x5, starting transfers between devices, passed_along(): lax.ppermute(value, axis, [(i, (i + by) % peers) for i in range(peers)])  12.5 us
    unnamed x15, local copies, waits for them, and re-layouts  10.1 us
  transfers between devices with their start and end apart: 7, of which 6 were waited for; matrix products, arithmetic and copies ran while one was open for 1% of the time, Pallas kernels for 0%

profile of v1, /device:TPU:0, one launch (start us, length us, event | category | flops | bytes accessed | tf_op | source)
XLA Modules:
  0.0 210.6 jit_solution(11763186594943374443)
XLA Ops:
  7.2 0.0 all-reduce.5.cloned.1.call-start
  7.2 3.0 %collective-permute-start = (f32[2,256,256]{2,1,0:T(8,128)}, f32[2,256,256]{2,1,0:T(8,128)S(1)}, u32[]{:S(2)}, u32[]{:S(2)}) collective-permute-start(f32[2,256,256]{2,1,0:T(8,128)} %own_ref.1), channel_id=1, source_target_pairs={{0,2},{2,0},{1,3},{3,1},{4,6},{6,4},{5,7},{7,5},{8,10},{10,8},{9,1... | collective-permute-start | bytes 1572872 | tf_op jit(solution)/shard_map/ppermute | solution.py:14
  10.2 3.6 %collective-permute-start.1 = (f32[2,256,256]{2,1,0:T(8,128)}, f32[2,256,256]{2,1,0:T(8,128)S(1)}, u32[]{:S(2)}, u32[]{:S(2)}) collective-permute-start(f32[2,256,256]{2,1,0:T(8,128)} %own_ref.1), channel_id=1, source_target_pairs={{0,12},{4,0},{8,4},{12,8},{1,13},{5,1},{9,5},{13,9},{2,14},{6,2},{... | collective-permute-start | bytes 1572872 | tf_op jit(solution)/shard_map/ppermute | solution.py:14
  13.8 8.5 %collective-permute-done.right_ref = f32[2,256,256]{2,1,0:T(8,128)S(1)} collective-permute-done((f32[2,256,256]{2,1,0:T(8,128)}, f32[2,256,256]{2,1,0:T(8,128)S(1)}, u32[]{:S(2)}, u32[]{:S(2)}) %collective-permute-start) | collective-permute-done | bytes 524320 | tf_op jit(solution)/shard_map/ppermute | solution.py:14
  22.3 3.8 %collective-permute-start.2 = (f32[2,256,256]{2,1,0:T(8,128)S(1)}, f32[2,256,256]{2,1,0:T(8,128)S(1)}, u32[]{:S(2)}, u32[]{:S(2)}) collective-permute-start(f32[2,256,256]{2,1,0:T(8,128)S(1)} %collective-permute-done.right_ref), channel_id=1, source_target_pairs={{0,12},{4,0},{8,4},{12,8},{1,13},{5,1},{9,5},{13,9},{2,14},{6,2},{... | collective-permute-start | bytes 1572872 | tf_op jit(solution)/shard_map/ppermute | solution.py:14
  26.9 0.8 copy.9.pos_ref
  27.6 0.0 collective-permute-done.1.down_ref
  27.6 8.9 %collective-permute-done.2.diag_ref = f32[2,256,256]{2,1,0:T(8,128)S(1)} collective-permute-done((f32[2,256,256]{2,1,0:T(8,128)S(1)}, f32[2,256,256]{2,1,0:T(8,128)S(1)}, u32[]{:S(2)}, u32[]{:S(2)}) %collective-permute-start.2) | collective-permute-done | bytes 524320 | tf_op jit(solution)/shard_map/ppermute | solution.py:14
  36.5 0.0 copy-start
  36.5 1.4 copy-done
  37.9 1.2 copy-done.1
  39.1 1.0 copy-done.2
  40.2 1.0 copy-done.3
  41.2 0.9 copy-done.4
  42.1 16.7 %shard_map.86 = (f32[4,2,256,256]{3,2,1,0:T(8,128)}, f32[2,256,256]{2,1,0:T(8,128)}) custom-call(s32[6,2]{1,0:T(8,128)S(1)} %copy.9.pos_ref, s32[1]{0:T(128)S(6)} %copy.12.cnt_ref, f32[2,256,256]{2,1,0:T(8,128)S(1)} %copy-done.2, f32[2,256,256]{2,1,0:T(8,128)S(1)} %collective-permute-done.right_ref, f32[2,256,256]{2,1,0:T(8,128)S(1)} %collective-permute-done.1.down_ref, ...), custom_call_target="tpu_custom_call" | custom-call | tf_op jit(solution)/shard_map/pallas_call | solution.py:195
  58.8 0.0 copy-start.5
  58.8 1.4 fusion.3
  60.3 0.1 pad_maximum_fusion
  60.3 1.6 collective-permute-start.3
  61.9 21.6 %collective-permute-done.3 = f32[2,2,256,256]{3,2,1,0:T(8,128)S(1)} collective-permute-done((f32[2,2,256,256]{3,2,1,0:T(8,128)S(1)}, f32[2,2,256,256]{3,2,1,0:T(8,128)S(1)}, u32[]{:S(2)}, u32[]{:S(2)}) %collective-permute-start.3) | collective-permute-done | bytes 1048608 | tf_op jit(solution)/shard_map/ppermute | solution.py:14
  83.5 0.0 copy-done.5
  83.5 0.9 fusion
  84.4 0.5 collective-permute-start.4
  84.8 0.0 all-reduce.5.cloned.1.call-update
  84.9 0.0 all-reduce.3.cloned.1.call-start
  84.9 13.8 %collective-permute-done.4 = f32[2,256,256]{2,1,0:T(8,128)} collective-permute-done((f32[2,256,256]{2,1,0:T(8,128)}, f32[2,256,256]{2,1,0:T(8,128)}, u32[]{:S(2)}, u32[]{:S(2)}) %collective-permute-start.4) | collective-permute-done | bytes 524320 | tf_op jit(solution)/shard_map/ppermute | solution.py:14
  98.8 1.9 fusion.2
  100.7 0.0 all-reduce.3.cloned.1.call-update
  100.7 77.2 %all-reduce.5.cloned.1.call-done = f32[2,256,256]{2,1,0:T(8,128)} async-done(((f32[2,256,256]{2,1,0:T(8,128)}), f32[2,256,256]{2,1,0:T(8,128)}) %all-reduce.5.cloned.1.call-update) | async-done | bytes 524304 | tf_op jit(solution)/shard_map/psum | solution.py:213
  177.9 22.2 %all-reduce.3.cloned.1.call-done = f32[2,256,256]{2,1,0:T(8,128)} async-done(((f32[2,256,256]{2,1,0:T(8,128)}), f32[2,256,256]{2,1,0:T(8,128)}) %all-reduce.3.cloned.1.call-update) | async-done | bytes 524304 | tf_op jit(solution)/shard_map/psum | solution.py:216
  200.1 1.9 copy.13
  201.9 1.9 copy.14
  (4 shorter events, 0.0 us)
Async XLA Ops:
  7.2 170.7 %all-reduce.5.cloned.1.call-start = ((), (), s32[]{:S(2)}) async-start(), calls=%async_computation.1 | async-start | bytes 1048576 | tf_op jit(solution)/shard_map/psum | solution.py:213
  7.2 15.1 %collective-permute-start = (f32[2,256,256]{2,1,0:T(8,128)}, f32[2,256,256]{2,1,0:T(8,128)S(1)}, u32[]{:S(2)}, u32[]{:S(2)}) collective-permute-start(f32[2,256,256]{2,1,0:T(8,128)} %own_ref.1), channel_id=1, source_target_pairs={{0,2},{2,0},{1,3},{3,1},{4,6},{6,4},{5,7},{7,5},{8,10},{10,8},{9,1... | collective-permute-start | bytes 1572872 | tf_op jit(solution)/shard_map/ppermute | solution.py:14
  10.2 17.4 %collective-permute-start.1 = (f32[2,256,256]{2,1,0:T(8,128)}, f32[2,256,256]{2,1,0:T(8,128)S(1)}, u32[]{:S(2)}, u32[]{:S(2)}) collective-permute-start(f32[2,256,256]{2,1,0:T(8,128)} %own_ref.1), channel_id=1, source_target_pairs={{0,12},{4,0},{8,4},{12,8},{1,13},{5,1},{9,5},{13,9},{2,14},{6,2},{... | collective-permute-start | bytes 1572872 | tf_op jit(solution)/shard_map/ppermute | solution.py:14
  22.3 14.2 %collective-permute-start.2 = (f32[2,256,256]{2,1,0:T(8,128)S(1)}, f32[2,256,256]{2,1,0:T(8,128)S(1)}, u32[]{:S(2)}, u32[]{:S(2)}) collective-permute-start(f32[2,256,256]{2,1,0:T(8,128)S(1)} %collective-permute-done.right_ref), channel_id=1, source_target_pairs={{0,12},{4,0},{8,4},{12,8},{1,13},{5,1},{9,5},{13,9},{2,14},{6,2},{... | collective-permute-start | bytes 1572872 | tf_op jit(solution)/shard_map/ppermute | solution.py:14
  36.5 1.4 copy-start
  37.9 1.2 copy-start.1
  39.1 1.0 copy-start.2
  40.2 1.0 copy-start.3
  41.2 0.9 copy-start.4
  58.8 24.7 %copy-start.5 = (f32[4,2,256,256]{3,2,1,0:T(8,128)S(1)}, f32[4,2,256,256]{3,2,1,0:T(8,128)}, u32[]{:S(2)}) copy-start(f32[4,2,256,256]{3,2,1,0:T(8,128)} %get-tuple-element.4) | copy-start | bytes 6291460
  60.3 23.2 %collective-permute-start.3 = (f32[2,2,256,256]{3,2,1,0:T(8,128)S(1)}, f32[2,2,256,256]{3,2,1,0:T(8,128)S(1)}, u32[]{:S(2)}, u32[]{:S(2)}) collective-permute-start(f32[2,2,256,256]{3,2,1,0:T(8,128)S(1)} %pad_maximum_fusion), channel_id=1, source_target_pairs={{0,2},{2,0},{1,3},{3,1},{4,6},{6,4},{5,7},{7,5},{8,10},{10,8},{9,1... | collective-permute-start | bytes 3145736 | tf_op jit(solution)/shard_map/ppermute | solution.py:14
  84.4 14.4 %collective-permute-start.4 = (f32[2,256,256]{2,1,0:T(8,128)}, f32[2,256,256]{2,1,0:T(8,128)}, u32[]{:S(2)}, u32[]{:S(2)}) collective-permute-start(f32[2,256,256]{2,1,0:T(8,128)} %fusion), channel_id=1, source_target_pairs={{0,4},{4,8},{8,12},{12,0},{1,5},{5,9},{9,13},{13,1},{2,6},{6,10},{... | collective-permute-start | bytes 1572872 | tf_op jit(solution)/shard_map/ppermute | solution.py:14
  84.9 115.2 %all-reduce.3.cloned.1.call-start = ((), (), s32[]{:S(2)}) async-start(), calls=%async_computation | async-start | bytes 1048576 | tf_op jit(solution)/shard_map/psum | solution.py:216
Sparse Core Ops, SparseCore 0:
  85.0 92.8 all-reduce.4
  180.8 19.2 all-reduce.2

commit v2 on v1

v2 whole, which is shorter than its diff:
```python
import jax
import jax.numpy as jnp
import numpy as np
from jax import lax
from jax.experimental import pallas as pl
from jax.experimental.pallas import tpu as pltpu
from jax.sharding import PartitionSpec as P


def half_tables(size):
    half = size // 2
    pixel = np.arange(half)
    tables = []
    for parity in (0, 1):
        freq = 2 * np.arange(half) + parity
        phase = (freq[:, None] * pixel[None, :] % size) * (2.0 * np.pi / size)
        cos_tab = np.cos(phase) / np.sqrt(size)
        sin_tab = np.sin(phase) / np.sqrt(size)
        full = np.block([[cos_tab, sin_tab], [-sin_tab, cos_tab]])
        tables += [full, full.T]
    full = np.stack(tables)
    high = full.astype(jnp.bfloat16)
    low = (full - high.astype(np.float64)).astype(jnp.bfloat16)
    return np.stack([high, low], axis=1)


def order_table(size):
    order = np.concatenate([np.arange(0, size, 2), np.arange(1, size, 2)])
    table = np.zeros((size, size), np.float32)
    table[order, np.arange(size)] = 1.0
    return table.astype(jnp.bfloat16)


def split(value):
    high = value.astype(jnp.bfloat16)
    low = (value - high.astype(jnp.float32)).astype(jnp.bfloat16)
    return high, low


def mm(left, right):
    return jnp.dot(left, right, preferred_element_type=jnp.float32)


def left_product(tab_ref, which, value):
    high, low = split(value)
    return mm(tab_ref[which, 0], high) + mm(tab_ref[which, 0], low) + mm(tab_ref[which, 1], high)


def right_product(tab_ref, which, value):
    high, low = split(value)
    return mm(high, tab_ref[which, 0]) + mm(low, tab_ref[which, 0]) + mm(high, tab_ref[which, 1])


def forward(re, im, tab_ref):
    half = re.shape[0] // 2
    cat = jnp.concatenate
    even = cat([re[:half] + re[half:], im[:half] + im[half:]], 0)
    odd = cat([re[:half] - re[half:], im[:half] - im[half:]], 0)
    even = left_product(tab_ref, 0, even)
    odd = left_product(tab_ref, 2, odd)
    re = cat([even[:half], odd[:half]], 0)
    im = cat([even[half:], odd[half:]], 0)
    even = cat([re[:, :half] + re[:, half:], im[:, :half] + im[:, half:]], 1)
    odd = cat([re[:, :half] - re[:, half:], im[:, :half] - im[:, half:]], 1)
    even = right_product(tab_ref, 1, even)
    odd = right_product(tab_ref, 3, odd)
    return cat([even[:, :half], odd[:, :half]], 1), cat([even[:, half:], odd[:, half:]], 1)


def backward(re, im, tab_ref):
    half = re.shape[0] // 2
    cat = jnp.concatenate
    even = right_product(tab_ref, 0, cat([re[:, :half], im[:, :half]], 1))
    odd = right_product(tab_ref, 2, cat([re[:, half:], im[:, half:]], 1))
    total, diff = even + odd, even - odd
    re = cat([total[:, :half], diff[:, :half]], 1)
    im = cat([total[:, half:], diff[:, half:]], 1)
    even = left_product(tab_ref, 1, cat([re[:half], im[:half]], 0))
    odd = left_product(tab_ref, 3, cat([re[half:], im[half:]], 0))
    total, diff = even + odd, even - odd
    return cat([total[:half], diff[:half]], 0), cat([total[half:], diff[half:]], 0)


def rolled(value, rows, cols):
    return pltpu.roll(pltpu.roll(value, rows, 0), cols, 1)


MESH = pl.DeviceIdType.MESH
TILE_PARTS = 2
GRAD_PARTS = 4


def kernel(
    pos_ref, cnt_ref, own_ref, probe_ref, amp_ref, tab_ref, ord_ref,
    grad_ref, pgrad_ref,
    tiles, turned, ordered, held, columns, quads, sibs, arrived, pacc, psib, px_buf, py_buf,
    amp_sem, tile_send, tile_recv, pass_send, pass_recv, sib_send, sib_recv, far_send, far_recv,
    out_send, out_recv, ps_send, ps_recv, px_send, px_recv, py_send, py_recv,
    gy_send, gy_recv, gx_send, gx_recv, po_send, po_recv,
):
    slots, size = amp_ref.shape[0], amp_ref.shape[1]
    half = size // 2
    lanes = columns.shape[0]
    tx, ty, pz = lax.axis_index("tx"), lax.axis_index("ty"), lax.axis_index("pz")
    ntx, nty = lax.axis_size("tx"), lax.axis_size("ty")
    other = 1 - pz

    def at(dy, dx):
        return {"ty": lax.rem(ty + dy + nty, nty), "tx": lax.rem(tx + dx + ntx, ntx)}

    def send(src, dst, send_sem, recv_sem, device):
        copy = pltpu.make_async_remote_copy(
            src_ref=src, dst_ref=dst, send_sem=send_sem, recv_sem=recv_sem,
            device_id=device, device_id_type=MESH,
        )
        copy.start()
        return copy

    amp_copies = [
        pltpu.make_async_copy(
            amp_ref.at[:, :, pl.ds(part * 128, 128)], columns.at[part], amp_sem.at[part]
        )
        for part in range(lanes)
    ]
    for copy in amp_copies:
        copy.start()

    partners = [{"pz": other}, at(-1, -1), at(1, 1)]
    partners += [at(0, d) for d in range(1, ntx)] + [at(d, 0) for d in range(1, nty)]
    barrier = pltpu.get_barrier_semaphore()
    for partner in partners:
        pl.semaphore_signal(barrier, inc=1, device_id=partner, device_id_type=MESH)
    pl.semaphore_wait(barrier, len(partners))

    waits = []
    part_rows = size // TILE_PARTS
    tile_copies = []
    for part in range(TILE_PARTS):
        rows = pl.ds(part * part_rows, part_rows)
        for quad, device in enumerate((at(0, -1), at(-1, 0), at(-1, -1))):
            tile_copies.append((quad, part, send(
                own_ref.at[pz, rows], tiles.at[quad, pz, rows],
                tile_send.at[quad, part], tile_recv.at[quad, part], device,
            )))

    row_id = lax.broadcasted_iota(jnp.int32, (size, size), 0)
    col_id = lax.broadcasted_iota(jnp.int32, (size, size), 1)
    row_base, col_base = ty * size, tx * size
    used_count = cnt_ref[0]
    for copy in amp_copies:
        copy.wait()

    def prepare(slot, carry):
        row = pos_ref[slot, 0] - row_base
        col = pos_ref[slot, 1] - col_base
        for p in range(2):
            turned[slot, p] = rolled(probe_ref[p], row, col)
        amp = jnp.concatenate(
            [
                jnp.concatenate(
                    [columns[part, slot, pl.ds(parity, half, 2), :] for part in range(lanes)], 1
                )
                for parity in (0, 1)
            ],
            0,
        )
        high, low = split(amp)
        ordered[slot] = mm(high, ord_ref[...]) + mm(low, ord_ref[...])
        return carry

    lax.fori_loop(0, slots, prepare, 0)
    pacc[...] = jnp.zeros_like(pacc)

    pass_copies = []
    for quad, part, copy in tile_copies:
        copy.wait_recv()
        rows = pl.ds(part * part_rows, part_rows)
        pass_copies.append(send(
            tiles.at[quad, pz, rows], tiles.at[quad, pz, rows],
            pass_send.at[quad, part], pass_recv.at[quad, part], {"pz": other},
        ))
        waits += [copy, pass_copies[-1]]
    for copy in pass_copies:
        copy.wait_recv()

    def visit(slot, carry):
        row = pos_ref[slot, 0] - row_base
        col = pos_ref[slot, 1] - col_base
        used = (slot < used_count).astype(jnp.float32)
        above = row_id < row
        before = col_id < col
        patch = [
            jnp.where(
                above,
                jnp.where(before, tiles[2, p], tiles[1, p]),
                jnp.where(before, tiles[0, p], own_ref[p]),
            )
            for p in range(2)
        ]
        probe = [turned[slot, p] for p in range(2)]
        exit_re = probe[0] * patch[0] - probe[1] * patch[1]
        exit_im = probe[0] * patch[1] + probe[1] * patch[0]
        far_re, far_im = forward(exit_re, exit_im, tab_ref)
        gain = used * (1.0 - ordered[slot] * lax.rsqrt(far_re * far_re + far_im * far_im + 0.01))
        back_re, back_im = backward(far_re * gain, far_im * gain, tab_ref)
        held[slot, 0] = probe[0] * back_re + probe[1] * back_im
        held[slot, 1] = probe[0] * back_im - probe[1] * back_re
        up, left = lax.rem(size - row, size), lax.rem(size - col, size)
        pacc[0] += rolled(patch[0] * back_re + patch[1] * back_im, up, left)
        pacc[1] += rolled(patch[0] * back_im - patch[1] * back_re, up, left)
        return carry

    lax.fori_loop(0, slots, visit, 0)

    probe_copy = send(pacc.at[other], psib, ps_send, ps_recv, {"pz": other})

    chunk = 16
    part_rows = size // GRAD_PARTS
    sib_copies = []
    for part in range(GRAD_PARTS):

        def collect(step, carry):
            base = pl.multiple_of(part * part_rows + step * chunk, chunk)
            row_part = base + lax.broadcasted_iota(jnp.int32, (chunk, size), 0)
            col_part = lax.broadcasted_iota(jnp.int32, (chunk, size), 1)
            for p in range(2):
                sums = [jnp.zeros((chunk, size), jnp.float32) for _ in range(4)]
                for slot in range(slots):
                    above = row_part < pos_ref[slot, 0] - row_base
                    before = col_part < pos_ref[slot, 1] - col_base
                    piece = held[slot, p, pl.ds(base, chunk), :]
                    low = jnp.where(above, piece, 0.0)
                    top = piece - low
                    low_left = jnp.where(before, low, 0.0)
                    top_left = jnp.where(before, top, 0.0)
                    sums = [
                        sums[0] + (top - top_left),
                        sums[1] + top_left,
                        sums[2] + (low - low_left),
                        sums[3] + low_left,
                    ]
                for quad in range(4):
                    quads[quad, p, pl.ds(base, chunk), :] = sums[quad]
            return carry

        lax.fori_loop(0, part_rows // chunk, collect, 0)
        rows = pl.ds(part * part_rows, part_rows)
        sib_copies.append(send(
            quads.at[:, other, rows], sibs.at[:, rows],
            sib_send.at[part], sib_recv.at[part], {"pz": other},
        ))

    far_copies = []
    for part in range(GRAD_PARTS):
        rows = pl.ds(part * part_rows, part_rows)
        sib_copies[part].wait_recv()
        for quad in range(4):
            quads[quad, pz, rows, :] += sibs[quad, rows, :]
        for quad, device in enumerate((at(0, 1), at(1, 0), at(1, 1))):
            far_copies.append(send(
                quads.at[quad + 1, pz, rows], arrived.at[quad, rows],
                far_send.at[quad, part], far_recv.at[quad, part], device,
            ))

    probe_copy.wait_recv()
    pacc[pz] += psib[...]
    base, count = 0, size
    levels = []
    for axis, peers, me, buf, sends, recvs in (
        ("tx", ntx, tx, px_buf, px_send, px_recv), ("ty", nty, ty, py_buf, py_send, py_recv)
    ):
        scatter = count // peers >= 8
        piece = count // peers if scatter else count
        copies = []
        for d in range(1, peers):
            peer = lax.rem(me + d, peers)
            start = pl.multiple_of(base + peer * piece, 8) if scatter else base
            copies.append(send(
                pacc.at[pz, pl.ds(start, piece)], buf.at[d - 1, pl.ds(0, piece)],
                sends.at[d - 1], recvs.at[d - 1], {axis: peer},
            ))
        base = pl.multiple_of(base + me * piece, 8) if scatter else base
        for copy in copies:
            copy.wait()
        total = pacc[pz, pl.ds(base, piece), :]
        for d in range(1, peers):
            total += buf[d - 1, pl.ds(0, piece), :]
        pacc[pz, pl.ds(base, piece), :] = total
        count = piece
        levels.append((axis, peers, me, scatter, base, piece))
    pgrad_ref[pz, pl.ds(base, count), :] = pacc[pz, pl.ds(base, count), :]
    for (axis, peers, me, scatter, base, piece), sends, recvs in zip(
        levels[::-1], (gy_send, gx_send), (gy_recv, gx_recv)
    ):
        if scatter:
            copies = [
                send(
                    pgrad_ref.at[pz, pl.ds(base, piece)], pgrad_ref.at[pz, pl.ds(base, piece)],
                    sends.at[d - 1], recvs.at[d - 1], {axis: lax.rem(me + d, peers)},
                )
                for d in range(1, peers)
            ]
            for copy in copies:
                copy.wait()
    last = send(pgrad_ref.at[pz], pgrad_ref.at[pz], po_send, po_recv, {"pz": other})

    out_copies = []
    for part in range(GRAD_PARTS):
        rows = pl.ds(part * part_rows, part_rows)
        for copy in far_copies[3 * part : 3 * part + 3]:
            copy.wait_recv()
        grad_ref[pz, rows, :] = (
            quads[0, pz, rows, :] + arrived[0, rows, :] + arrived[1, rows, :] + arrived[2, rows, :]
        )
        out_copies.append(send(
            grad_ref.at[pz, rows], grad_ref.at[pz, rows],
            out_send.at[part], out_recv.at[part], {"pz": other},
        ))
    for copy in out_copies + [last]:
        copy.wait()
    for copy in waits + sib_copies + far_copies + [probe_copy]:
        copy.wait_send()


def per_device(object_field, probe_wave, amplitudes, positions, counts):
    size = probe_wave.shape[1]
    slots = positions.shape[0]
    ntx, nty = lax.axis_size("tx"), lax.axis_size("ty")
    vmem = pl.BlockSpec(memory_space=pltpu.VMEM)
    smem = pl.BlockSpec(memory_space=pltpu.SMEM)
    x_piece = size // ntx if size // ntx >= 8 else size
    y_piece = x_piece // nty if x_piece // nty >= 8 else x_piece
    plane = (size, size)
    dma = pltpu.SemaphoreType.DMA

    def buffer(*shape):
        return pltpu.VMEM(shape, jnp.float32)

    lanes = size // 128
    pairs = [(3, TILE_PARTS)] * 2 + [(GRAD_PARTS,), (3, GRAD_PARTS), (GRAD_PARTS,), None]
    pairs += [(ntx - 1,), (nty - 1,), (nty - 1,), (ntx - 1,), None]
    sems = [dma((lanes,))]
    for shape in pairs:
        sems += [dma(shape) if shape else dma] * 2
    return pl.pallas_call(
        kernel,
        out_shape=(
            jax.ShapeDtypeStruct((2,) + plane, jnp.float32),
            jax.ShapeDtypeStruct((2,) + plane, jnp.float32),
        ),
        in_specs=[smem, smem, vmem, vmem, pl.BlockSpec(memory_space=pl.ANY), vmem, vmem],
        out_specs=(vmem, vmem),
        scratch_shapes=[
            buffer(3, 2, *plane),
            buffer(slots, 2, *plane),
            buffer(slots, *plane),
            buffer(slots, 2, *plane),
            buffer(lanes, slots, size, 128),
            buffer(4, 2, *plane),
            buffer(4, *plane),
            buffer(3, *plane),
            buffer(2, *plane),
            buffer(*plane),
            buffer(ntx - 1, x_piece, size),
            buffer(nty - 1, y_piece, size),
        ] + sems,
        compiler_params=pltpu.CompilerParams(
            vmem_limit_bytes=48 * 1024 * 1024, collective_id=0, has_side_effects=True
        ),
    )(
        positions, counts, object_field, probe_wave, amplitudes,
        jnp.asarray(half_tables(size)), jnp.asarray(order_table(size)),
    )


def solution(mesh):
    return jax.shard_map(
        per_device,
        mesh=mesh,
        in_specs=(
            P(None, ("groups", "ty"), "tx"),
            P(),
            P(("groups", "ty", "tx", "pz"), None, None),
            P(("groups", "ty", "tx", "pz"), None),
            P(("groups", "ty", "tx", "pz")),
        ),
        out_specs=(P(None, ("groups", "ty"), "tx"), P("groups", None, None)),
        check_vma=False,
    )
```

time: 211 us -> 74 us (0.35)
  waiting for transfers between devices: 152 us -> 0 us
  Pallas kernels: 16.7 us -> 64.4 us
  between operations: 14.7 us -> 1.29 us
  starting transfers between devices: 12.5 us -> 0 us
  local copies, waits for them, and re-layouts: 11.6 us -> 7.97 us
  other arithmetic: 2.88 us -> 0 us
    psum x2 -> x0, waiting for transfers between devices: 99.4 us -> none  [the longest x1 77.2 us: per_device(): probe_grad = lax.psum(probe_part, ('ty', 'tx', 'pz'))]
    ppermute x5 -> x0, waiting for transfers between devices: 52.9 us -> none  [passed_along(): lax.ppermute(value, axis, [(i, (i + by) % peers) for i in range(peers)])]
    pallas_call x1, Pallas kernels: 16.7 us -> 64.4 us  [per_device(): pl.pallas_call(kernel, out_shape=(jax.ShapeDtypeStruct((2,) + plane, jnp....]
    ppermute x5 -> x0, starting transfers between devices: 12.5 us -> none  [passed_along(): lax.ppermute(value, axis, [(i, (i + by) % peers) for i in range(peers)])]
    add x2 -> x0, other arithmetic: 2.79 us -> none  [the longest x1 1.93 us: per_device(): object_grad = lax.psum(grads[0] + from_right[0] + from_down, 'pz')]
    unnamed x15 -> x13, local copies, waits for them, and re-layouts: 10.1 us -> 7.97 us
  transfers between devices with their start and end apart: 7 -> 0, of which waited for: 6 -> 0; matrix products, arithmetic and copies ran while one was open for 1% -> 0% of each run, Pallas kernels for 0% -> 0%
where the time goes in v2:
time: 74 us; the launch traced here: 73.7 us
  Pallas kernels  64.4 us (87%)
  local copies, waits for them, and re-layouts  7.97 us (11%)
  between operations  1.29 us (2%)
    pallas_call x1, Pallas kernels, per_device(): pl.pallas_call(kernel, out_shape=(jax.ShapeDtypeStruct((2,) + plane, jnp....  64.4 us
    unnamed x13, local copies, waits for them, and re-layouts  7.97 us

profile of v2, /device:TPU:0, one launch (start us, length us, event | category | flops | bytes accessed | tf_op | source)
XLA Modules:
  0.0 73.7 jit_solution(3864886675485514861)
XLA Ops:
  1.3 0.8 %copy.9.pos_ref = s32[6,2]{1,0:T(8,128)S(1)} copy(s32[6,2]{0,1:T(2,128)} %param.10) | data formatting | bytes 96 | tf_op args[3]
  2.0 0.0 copy-start
  2.0 1.4 %copy-done = f32[6,256,256]{2,1,0:T(8,128)S(1)} copy-done((f32[6,256,256]{2,1,0:T(8,128)S(1)}, f32[6,256,256]{2,1,0:T(8,128)}, u32[]{:S(2)}) %copy-start) | copy-done | bytes 1572888
  3.5 0.0 copy-start.1
  3.5 1.2 %copy-done.1 = bf16[4,2,256,256]{3,2,1,0:T(8,128)(2,1)S(1)} copy-done((bf16[4,2,256,256]{3,2,1,0:T(8,128)(2,1)S(1)}, bf16[4,2,256,256]{3,2,1,0:T(8,128)(2,1)}, u32[]{:S(2)}) %copy-start.1) | copy-done | bytes 1048600
  4.7 0.0 copy-start.2
  4.7 1.0 %copy-done.2 = f32[2,256,256]{2,1,0:T(8,128)S(1)} copy-done((f32[2,256,256]{2,1,0:T(8,128)S(1)}, f32[2,256,256]{2,1,0:T(8,128)}, u32[]{:S(2)}) %copy-start.2) | copy-done | bytes 524312
  5.7 0.0 copy-start.3
  5.7 1.0 %copy-done.3 = f32[2,256,256]{2,1,0:T(8,128)S(1)} copy-done((f32[2,256,256]{2,1,0:T(8,128)S(1)}, f32[2,256,256]{2,1,0:T(8,128)}, u32[]{:S(2)}) %copy-start.3) | copy-done | bytes 524312
  6.8 0.0 copy-start.4
  6.8 0.9 %copy-done.4 = bf16[256,256]{1,0:T(8,128)(2,1)S(1)} copy-done((bf16[256,256]{1,0:T(8,128)(2,1)S(1)}, bf16[256,256]{1,0:T(8,128)(2,1)}, u32[]{:S(2)}) %copy-start.4) | copy-done | bytes 131096
  7.7 64.4 %shard_map.86 = (f32[2,256,256]{2,1,0:T(8,128)S(1)}, f32[2,256,256]{2,1,0:T(8,128)S(1)}) custom-call(s32[6,2]{1,0:T(8,128)S(1)} %copy.9.pos_ref, s32[1]{0:T(128)S(6)} %copy.12.cnt_ref, f32[2,256,256]{2,1,0:T(8,128)S(1)} %copy-done.2, f32[2,256,256]{2,1,0:T(8,128)S(1)} %copy-done.3, f32[6,256,256]{2,1,0:T(8,128)S(1)} %copy-done, ...), custom_call_target="tpu_custom_call" | custom-call | tf_op jit(solution)/shard_map/pallas_call | solution.py:345
  72.1 0.8 %copy.13 = f32[2,256,256]{2,1,0:T(8,128)} copy(f32[2,256,256]{2,1,0:T(8,128)S(1)} %get-tuple-element.4) | data formatting | bytes 1048576
  72.9 0.8 %copy.14 = f32[2,256,256]{2,1,0:T(8,128)} copy(f32[2,256,256]{2,1,0:T(8,128)S(1)} %get-tuple-element.5) | data formatting | bytes 1048576
Async XLA Ops:
  2.0 1.4 %copy-start = (f32[6,256,256]{2,1,0:T(8,128)S(1)}, f32[6,256,256]{2,1,0:T(8,128)}, u32[]{:S(2)}) copy-start(f32[6,256,256]{2,1,0:T(8,128)} %amp_ref.1) | copy-start | bytes 4718596
  3.5 1.2 %copy-start.1 = (bf16[4,2,256,256]{3,2,1,0:T(8,128)(2,1)S(1)}, bf16[4,2,256,256]{3,2,1,0:T(8,128)(2,1)}, u32[]{:S(2)}) copy-start(bf16[4,2,256,256]{3,2,1,0:T(8,128)(2,1)} %constant.4.clone.tab_ref) | copy-start | bytes 3145732
  4.7 1.0 %copy-start.2 = (f32[2,256,256]{2,1,0:T(8,128)S(1)}, f32[2,256,256]{2,1,0:T(8,128)}, u32[]{:S(2)}) copy-start(f32[2,256,256]{2,1,0:T(8,128)} %own_ref.1) | copy-start | bytes 1572868
  5.7 1.0 %copy-start.3 = (f32[2,256,256]{2,1,0:T(8,128)S(1)}, f32[2,256,256]{2,1,0:T(8,128)}, u32[]{:S(2)}) copy-start(f32[2,256,256]{2,1,0:T(8,128)} %probe_ref.1) | copy-start | bytes 1572868
  6.8 0.9 %copy-start.4 = (bf16[256,256]{1,0:T(8,128)(2,1)S(1)}, bf16[256,256]{1,0:T(8,128)(2,1)}, u32[]{:S(2)}) copy-start(bf16[256,256]{1,0:T(8,128)(2,1)} %constant.5.clone.ord_ref) | copy-start | bytes 393220

commit v3 on v2

--- a/solution.py
+++ b/solution.py
@@ -91,9 +91,9 @@
 
 
 def kernel(
-    pos_ref, cnt_ref, own_ref, probe_ref, amp_ref, tab_ref, ord_ref,
+    pos_ref, cnt_ref, own_hbm, probe_hbm, amp_ref, tab_hbm, ord_hbm,
     grad_ref, pgrad_ref,
-    tiles, turned, ordered, held, columns, quads, sibs, arrived, pacc, psib, px_buf, py_buf,
+    own_ref, probe_ref, tab_ref, ord_ref, tiles, turned, ordered, held, columns, quads, sibs, arrived, pacc, psib, px_buf, py_buf,
     amp_sem, tile_send, tile_recv, pass_send, pass_recv, sib_send, sib_recv, far_send, far_recv,
     out_send, out_recv, ps_send, ps_recv, px_send, px_recv, py_send, py_recv,
     gy_send, gy_recv, gx_send, gx_recv, po_send, po_recv,
@@ -122,32 +122,56 @@
         )
         for part in range(lanes)
     ]
-    for copy in amp_copies:
-        copy.start()
-
-    partners = [{"pz": other}, at(-1, -1), at(1, 1)]
+    own_copy, probe_copy, tab_copy, ord_copy = [
+        pltpu.make_async_copy(src, dst, amp_sem.at[lanes + i])
+        for i, (src, dst) in enumerate(
+            ((own_hbm, own_ref), (probe_hbm, probe_ref), (tab_hbm, tab_ref), (ord_hbm, ord_ref))
+        )
+    ]
+
+    partners = [{"pz": other}]
     partners += [at(0, d) for d in range(1, ntx)] + [at(d, 0) for d in range(1, nty)]
     barrier = pltpu.get_barrier_semaphore()
     for partner in partners:
         pl.semaphore_signal(barrier, inc=1, device_id=partner, device_id_type=MESH)
+    for copy in [probe_copy, ord_copy] + amp_copies + [own_copy, tab_copy]:
+        copy.start()
     pl.semaphore_wait(barrier, len(partners))
 
     waits = []
     part_rows = size // TILE_PARTS
-    tile_copies = []
-    for part in range(TILE_PARTS):
-        rows = pl.ds(part * part_rows, part_rows)
-        for quad, device in enumerate((at(0, -1), at(-1, 0), at(-1, -1))):
-            tile_copies.append((quad, part, send(
-                own_ref.at[pz, rows], tiles.at[quad, pz, rows],
-                tile_send.at[quad, part], tile_recv.at[quad, part], device,
-            )))
+    up, left = at(-1, 0), at(0, -1)
+
+    def tile_rows(part):
+        return pl.ds(part * part_rows, part_rows)
+
+    def send_tile(src, quad, part, device):
+        copy = send(
+            src.at[tile_rows(part)], tiles.at[quad, pz, tile_rows(part)],
+            tile_send.at[quad, part], tile_recv.at[quad, part], device,
+        )
+        waits.append(copy)
+        return copy
+
+    def pass_on(quad, part):
+        copy = send(
+            tiles.at[quad, pz, tile_rows(part)], tiles.at[quad, pz, tile_rows(part)],
+            pass_send.at[quad, part], pass_recv.at[quad, part], {"pz": other},
+        )
+        waits.append(copy)
+        pass_copies.append(copy)
+
+    first = list(range(TILE_PARTS // 2))
+    second = list(range(TILE_PARTS // 2, TILE_PARTS))
+    pass_copies = []
+    right_copies = {part: send_tile(own_hbm.at[pz], 0, part, left) for part in first + second}
+    down_copies = {part: send_tile(own_hbm.at[pz], 1, part, up) for part in second + first}
 
     row_id = lax.broadcasted_iota(jnp.int32, (size, size), 0)
     col_id = lax.broadcasted_iota(jnp.int32, (size, size), 1)
     row_base, col_base = ty * size, tx * size
     used_count = cnt_ref[0]
-    for copy in amp_copies:
+    for copy in [probe_copy, ord_copy] + amp_copies:
         copy.wait()
 
     def prepare(slot, carry):
@@ -171,15 +195,24 @@
     lax.fori_loop(0, slots, prepare, 0)
     pacc[...] = jnp.zeros_like(pacc)
 
-    pass_copies = []
-    for quad, part, copy in tile_copies:
-        copy.wait_recv()
-        rows = pl.ds(part * part_rows, part_rows)
-        pass_copies.append(send(
-            tiles.at[quad, pz, rows], tiles.at[quad, pz, rows],
-            pass_send.at[quad, part], pass_recv.at[quad, part], {"pz": other},
-        ))
-        waits += [copy, pass_copies[-1]]
+    diag_copies = {}
+    for part_x, part_y in zip(first, second):
+        right_copies[part_x].wait_recv()
+        diag_copies[part_x] = send_tile(tiles.at[0, pz], 2, part_x, up)
+        down_copies[part_y].wait_recv()
+        diag_copies[part_y] = send_tile(tiles.at[1, pz], 2, part_y, left)
+        pass_on(0, part_x)
+        pass_on(1, part_y)
+    for part_x, part_y in zip(first, second):
+        right_copies[part_y].wait_recv()
+        pass_on(0, part_y)
+        down_copies[part_x].wait_recv()
+        pass_on(1, part_x)
+    for part in [part for pair in zip(first, second) for part in pair]:
+        diag_copies[part].wait_recv()
+        pass_on(2, part)
+    own_copy.wait()
+    tab_copy.wait()
     for copy in pass_copies:
         copy.wait_recv()
 
@@ -205,19 +238,21 @@
         back_re, back_im = backward(far_re * gain, far_im * gain, tab_ref)
         held[slot, 0] = probe[0] * back_re + probe[1] * back_im
         held[slot, 1] = probe[0] * back_im - probe[1] * back_re
-        up, left = lax.rem(size - row, size), lax.rem(size - col, size)
-        pacc[0] += rolled(patch[0] * back_re + patch[1] * back_im, up, left)
-        pacc[1] += rolled(patch[0] * back_im - patch[1] * back_re, up, left)
+        rows_back, cols_back = lax.rem(size - row, size), lax.rem(size - col, size)
+        pacc[0] += rolled(patch[0] * back_re + patch[1] * back_im, rows_back, cols_back)
+        pacc[1] += rolled(patch[0] * back_im - patch[1] * back_re, rows_back, cols_back)
         return carry
 
-    lax.fori_loop(0, slots, visit, 0)
+    lax.fori_loop(0, slots, visit, 0, unroll=slots)
 
     probe_copy = send(pacc.at[other], psib, ps_send, ps_recv, {"pz": other})
 
     chunk = 16
     part_rows = size // GRAD_PARTS
-    sib_copies = []
-    for part in range(GRAD_PARTS):
+    sib_copies = {}
+    half_parts = GRAD_PARTS // 2
+    order = [part + h * half_parts for part in range(half_parts) for h in (0, 1)]
+    for part in order:
 
         def collect(step, carry):
             base = pl.multiple_of(part * part_rows + step * chunk, chunk)
@@ -245,30 +280,37 @@
 
         lax.fori_loop(0, part_rows // chunk, collect, 0)
         rows = pl.ds(part * part_rows, part_rows)
-        sib_copies.append(send(
+        sib_copies[part] = send(
             quads.at[:, other, rows], sibs.at[:, rows],
             sib_send.at[part], sib_recv.at[part], {"pz": other},
-        ))
-
-    far_copies = []
-    for part in range(GRAD_PARTS):
+        )
+
+    far_copies = {}
+
+    def send_far(quad, slot, part, device):
+        rows = pl.ds(part * part_rows, part_rows)
+        far_copies[slot, part] = send(
+            quads.at[quad, pz, rows], arrived.at[slot, rows],
+            far_send.at[slot, part], far_recv.at[slot, part], device,
+        )
+
+    def send_first(part):
         rows = pl.ds(part * part_rows, part_rows)
         sib_copies[part].wait_recv()
         for quad in range(4):
             quads[quad, pz, rows, :] += sibs[quad, rows, :]
-        for quad, device in enumerate((at(0, 1), at(1, 0), at(1, 1))):
-            far_copies.append(send(
-                quads.at[quad + 1, pz, rows], arrived.at[quad, rows],
-                far_send.at[quad, part], far_recv.at[quad, part], device,
-            ))
-
-    probe_copy.wait_recv()
-    pacc[pz] += psib[...]
-    base, count = 0, size
-    levels = []
-    for axis, peers, me, buf, sends, recvs in (
-        ("tx", ntx, tx, px_buf, px_send, px_recv), ("ty", nty, ty, py_buf, py_send, py_recv)
-    ):
+        device = at(0, 1) if part < half_parts else at(1, 0)
+        send_far(3, 1, part, device)
+        send_far(1 if part < half_parts else 2, 0, part, device)
+
+    def send_second(part):
+        rows = pl.ds(part * part_rows, part_rows)
+        quad = 2 if part < half_parts else 1
+        far_copies[1, part].wait_recv()
+        quads[quad, pz, rows, :] += arrived[1, rows, :]
+        send_far(quad, 2, part, at(1, 0) if part < half_parts else at(0, 1))
+
+    def reduce_start(axis, peers, me, buf, sends, recvs, base, count):
         scatter = count // peers >= 8
         piece = count // peers if scatter else count
         copies = []
@@ -280,45 +322,69 @@
                 sends.at[d - 1], recvs.at[d - 1], {axis: peer},
             ))
         base = pl.multiple_of(base + me * piece, 8) if scatter else base
+        return copies, scatter, base, piece
+
+    def reduce_end(copies, buf, base, piece):
         for copy in copies:
             copy.wait()
         total = pacc[pz, pl.ds(base, piece), :]
-        for d in range(1, peers):
-            total += buf[d - 1, pl.ds(0, piece), :]
+        for d in range(len(copies)):
+            total += buf[d, pl.ds(0, piece), :]
         pacc[pz, pl.ds(base, piece), :] = total
-        count = piece
-        levels.append((axis, peers, me, scatter, base, piece))
-    pgrad_ref[pz, pl.ds(base, count), :] = pacc[pz, pl.ds(base, count), :]
-    for (axis, peers, me, scatter, base, piece), sends, recvs in zip(
-        levels[::-1], (gy_send, gx_send), (gy_recv, gx_recv)
-    ):
-        if scatter:
-            copies = [
-                send(
-                    pgrad_ref.at[pz, pl.ds(base, piece)], pgrad_ref.at[pz, pl.ds(base, piece)],
-                    sends.at[d - 1], recvs.at[d - 1], {axis: lax.rem(me + d, peers)},
-                )
-                for d in range(1, peers)
-            ]
-            for copy in copies:
-                copy.wait()
-    last = send(pgrad_ref.at[pz], pgrad_ref.at[pz], po_send, po_recv, {"pz": other})
+
+    def spread_start(axis, peers, me, sends, recvs, scatter, base, piece):
+        if not scatter:
+            return []
+        return [
+            send(
+                pgrad_ref.at[pz, pl.ds(base, piece)], pgrad_ref.at[pz, pl.ds(base, piece)],
+                sends.at[d - 1], recvs.at[d - 1], {axis: lax.rem(me + d, peers)},
+            )
+            for d in range(1, peers)
+        ]
+
+    probe_copy.wait_recv()
+    pacc[pz] += psib[...]
+    x_copies, x_scatter, x_base, x_piece = reduce_start(
+        "tx", ntx, tx, px_buf, px_send, px_recv, 0, size
+    )
+    for part in order[:2]:
+        send_first(part)
+    reduce_end(x_copies, px_buf, x_base, x_piece)
+    y_copies, y_scatter, y_base, y_piece = reduce_start(
+        "ty", nty, ty, py_buf, py_send, py_recv, x_base, x_piece
+    )
+    for part in order[2:]:
+        send_first(part)
+    for part in order[:2]:
+        send_second(part)
+    reduce_end(y_copies, py_buf, y_base, y_piece)
+    pgrad_ref[pz, pl.ds(y_base, y_piece), :] = pacc[pz, pl.ds(y_base, y_piece), :]
+    copies = spread_start("ty", nty, ty, gy_send, gy_recv, y_scatter, y_base, y_piece)
+    for part in order[2:]:
+        send_second(part)
+    for copy in copies:
+        copy.wait()
+    copies = spread_start("tx", ntx, tx, gx_send, gx_recv, x_scatter, x_base, x_piece)
 
     out_copies = []
-    for part in range(GRAD_PARTS):
+    for part in order:
         rows = pl.ds(part * part_rows, part_rows)
-        for copy in far_copies[3 * part : 3 * part + 3]:
-            copy.wait_recv()
-        grad_ref[pz, rows, :] = (
-            quads[0, pz, rows, :] + arrived[0, rows, :] + arrived[1, rows, :] + arrived[2, rows, :]
-        )
+        far_copies[0, part].wait_recv()
+        far_copies[2, part].wait_recv()
+        grad_ref[pz, rows, :] = quads[0, pz, rows, :] + arrived[0, rows, :] + arrived[2, rows, :]
         out_copies.append(send(
             grad_ref.at[pz, rows], grad_ref.at[pz, rows],
             out_send.at[part], out_recv.at[part], {"pz": other},
         ))
-    for copy in out_copies + [last]:
+    for copy in copies:
         copy.wait()
-    for copy in waits + sib_copies + far_copies + [probe_copy]:
+    out_copies.append(
+        send(pgrad_ref.at[pz], pgrad_ref.at[pz], po_send, po_recv, {"pz": other})
+    )
+    for copy in out_copies:
+        copy.wait()
+    for copy in waits + list(sib_copies.values()) + list(far_copies.values()) + [probe_copy]:
         copy.wait_send()
 
 
@@ -336,10 +402,11 @@
     def buffer(*shape):
         return pltpu.VMEM(shape, jnp.float32)
 
+    tables, ordering = jnp.asarray(half_tables(size)), jnp.asarray(order_table(size))
     lanes = size // 128
     pairs = [(3, TILE_PARTS)] * 2 + [(GRAD_PARTS,), (3, GRAD_PARTS), (GRAD_PARTS,), None]
     pairs += [(ntx - 1,), (nty - 1,), (nty - 1,), (ntx - 1,), None]
-    sems = [dma((lanes,))]
+    sems = [dma((lanes + 4,))]
     for shape in pairs:
         sems += [dma(shape) if shape else dma] * 2
     return pl.pallas_call(
@@ -348,9 +415,13 @@
             jax.ShapeDtypeStruct((2,) + plane, jnp.float32),
             jax.ShapeDtypeStruct((2,) + plane, jnp.float32),
         ),
-        in_specs=[smem, smem, vmem, vmem, pl.BlockSpec(memory_space=pl.ANY), vmem, vmem],
+        in_specs=[smem, smem] + [pl.BlockSpec(memory_space=pl.ANY)] * 5,
         out_specs=(vmem, vmem),
         scratch_shapes=[
+            buffer(2, *plane),
+            buffer(2, *plane),
+            pltpu.VMEM(tables.shape, tables.dtype),
+            pltpu.VMEM(ordering.shape, ordering.dtype),
             buffer(3, 2, *plane),
             buffer(slots, 2, *plane),
             buffer(slots, *plane),
@@ -369,7 +440,7 @@
         ),
     )(
         positions, counts, object_field, probe_wave, amplitudes,
-        jnp.asarray(half_tables(size)), jnp.asarray(order_table(size)),
+        tables, ordering,
     )
 
 

time: 74 us -> 60.1 us (0.81)
  Pallas kernels: 64.4 us -> 50.5 us
    pallas_call x1, Pallas kernels: 64.4 us -> 50.5 us  [per_device(): pl.pallas_call(kernel, out_shape=(jax.ShapeDtypeStruct((2,) + plane, jnp....]
where the time goes in v3:
time: 60.1 us; the launch traced here: 59.8 us
  Pallas kernels  50.5 us (84%)
  local copies, waits for them, and re-layouts  7.97 us (13%)
  between operations  1.29 us (2%)
    pallas_call x1, Pallas kernels, per_device(): pl.pallas_call(kernel, out_shape=(jax.ShapeDtypeStruct((2,) + plane, jnp....  50.5 us
    unnamed x13, local copies, waits for them, and re-layouts  7.97 us

profile of v3, /device:TPU:0, one launch (start us, length us, event | category | flops | bytes accessed | tf_op | source)
XLA Modules:
  0.0 59.8 jit_solution(3342127012321772914)
XLA Ops:
  1.3 0.8 %copy.9.pos_ref = s32[6,2]{1,0:T(8,128)S(1)} copy(s32[6,2]{0,1:T(2,128)} %param.10) | data formatting | bytes 96 | tf_op args[3]
  2.0 0.0 copy-start
  2.0 1.4 %copy-done = f32[6,256,256]{2,1,0:T(8,128)S(1)} copy-done((f32[6,256,256]{2,1,0:T(8,128)S(1)}, f32[6,256,256]{2,1,0:T(8,128)}, u32[]{:S(2)}) %copy-start) | copy-done | bytes 1572888
  3.5 0.0 copy-start.1
  3.5 1.2 %copy-done.1 = bf16[4,2,256,256]{3,2,1,0:T(8,128)(2,1)S(1)} copy-done((bf16[4,2,256,256]{3,2,1,0:T(8,128)(2,1)S(1)}, bf16[4,2,256,256]{3,2,1,0:T(8,128)(2,1)}, u32[]{:S(2)}) %copy-start.1) | copy-done | bytes 1048600
  4.7 0.0 copy-start.2
  4.7 1.0 %copy-done.2 = f32[2,256,256]{2,1,0:T(8,128)S(1)} copy-done((f32[2,256,256]{2,1,0:T(8,128)S(1)}, f32[2,256,256]{2,1,0:T(8,128)}, u32[]{:S(2)}) %copy-start.2) | copy-done | bytes 524312
  5.7 0.0 copy-start.3
  5.7 1.0 %copy-done.3 = f32[2,256,256]{2,1,0:T(8,128)S(1)} copy-done((f32[2,256,256]{2,1,0:T(8,128)S(1)}, f32[2,256,256]{2,1,0:T(8,128)}, u32[]{:S(2)}) %copy-start.3) | copy-done | bytes 524312
  6.8 0.0 copy-start.4
  6.8 0.9 %copy-done.4 = bf16[256,256]{1,0:T(8,128)(2,1)S(1)} copy-done((bf16[256,256]{1,0:T(8,128)(2,1)S(1)}, bf16[256,256]{1,0:T(8,128)(2,1)}, u32[]{:S(2)}) %copy-start.4) | copy-done | bytes 131096
  7.7 50.5 %shard_map.86 = (f32[2,256,256]{2,1,0:T(8,128)S(1)}, f32[2,256,256]{2,1,0:T(8,128)S(1)}) custom-call(s32[6,2]{1,0:T(8,128)S(1)} %copy.9.pos_ref, s32[1]{0:T(128)S(6)} %copy.12.cnt_ref, f32[2,256,256]{2,1,0:T(8,128)S(1)} %copy-done.2, f32[2,256,256]{2,1,0:T(8,128)S(1)} %copy-done.3, f32[6,256,256]{2,1,0:T(8,128)S(1)} %copy-done, ...), custom_call_target="tpu_custom_call" | custom-call | tf_op jit(solution)/shard_map/pallas_call | solution.py:412
  58.2 0.8 %copy.13 = f32[2,256,256]{2,1,0:T(8,128)} copy(f32[2,256,256]{2,1,0:T(8,128)S(1)} %get-tuple-element.4) | data formatting | bytes 1048576
  59.0 0.8 %copy.14 = f32[2,256,256]{2,1,0:T(8,128)} copy(f32[2,256,256]{2,1,0:T(8,128)S(1)} %get-tuple-element.5) | data formatting | bytes 1048576
Async XLA Ops:
  2.0 1.4 %copy-start = (f32[6,256,256]{2,1,0:T(8,128)S(1)}, f32[6,256,256]{2,1,0:T(8,128)}, u32[]{:S(2)}) copy-start(f32[6,256,256]{2,1,0:T(8,128)} %amp_ref.1) | copy-start | bytes 4718596
  3.5 1.2 %copy-start.1 = (bf16[4,2,256,256]{3,2,1,0:T(8,128)(2,1)S(1)}, bf16[4,2,256,256]{3,2,1,0:T(8,128)(2,1)}, u32[]{:S(2)}) copy-start(bf16[4,2,256,256]{3,2,1,0:T(8,128)(2,1)} %constant.4.clone.tab_hbm) | copy-start | bytes 3145732
  4.7 1.0 %copy-start.2 = (f32[2,256,256]{2,1,0:T(8,128)S(1)}, f32[2,256,256]{2,1,0:T(8,128)}, u32[]{:S(2)}) copy-start(f32[2,256,256]{2,1,0:T(8,128)} %own_hbm.1) | copy-start | bytes 1572868
  5.7 1.0 %copy-start.3 = (f32[2,256,256]{2,1,0:T(8,128)S(1)}, f32[2,256,256]{2,1,0:T(8,128)}, u32[]{:S(2)}) copy-start(f32[2,256,256]{2,1,0:T(8,128)} %probe_hbm.1) | copy-start | bytes 1572868
  6.8 0.9 %copy-start.4 = (bf16[256,256]{1,0:T(8,128)(2,1)S(1)}, bf16[256,256]{1,0:T(8,128)(2,1)}, u32[]{:S(2)}) copy-start(bf16[256,256]{1,0:T(8,128)(2,1)} %constant.5.clone.ord_hbm) | copy-start | bytes 393220

commit v4 on v3

--- a/solution.py
+++ b/solution.py
@@ -436,7 +436,7 @@
             buffer(nty - 1, y_piece, size),
         ] + sems,
         compiler_params=pltpu.CompilerParams(
-            vmem_limit_bytes=48 * 1024 * 1024, collective_id=0, has_side_effects=True
+            vmem_limit_bytes=62 * 1024 * 1024, collective_id=0, has_side_effects=True
         ),
     )(
         positions, counts, object_field, probe_wave, amplitudes,

time: 60.1 us -> 58.5 us (0.973)
  local copies, waits for them, and re-layouts: 7.97 us -> 5.09 us
  Pallas kernels: 50.5 us -> 51.9 us
    unnamed x13 -> x3, local copies, waits for them, and re-layouts: 7.97 us -> 5.09 us
    pallas_call x1, Pallas kernels: 50.5 us -> 51.9 us  [per_device(): pl.pallas_call(kernel, out_shape=(jax.ShapeDtypeStruct((2,) + plane, jnp....]
where the time goes in v4:
time: 58.5 us; the launch traced here: 58.2 us
  Pallas kernels  51.9 us (89%)
  local copies, waits for them, and re-layouts  5.09 us (9%)
  between operations  1.29 us (2%)
    pallas_call x1, Pallas kernels, per_device(): pl.pallas_call(kernel, out_shape=(jax.ShapeDtypeStruct((2,) + plane, jnp....  51.9 us
    unnamed x3, local copies, waits for them, and re-layouts  5.09 us

profile of v4, /device:TPU:0, one launch (start us, length us, event | category | flops | bytes accessed | tf_op | source)
XLA Modules:
  0.0 58.2 jit_solution(16114463812918483021)
XLA Ops:
  1.3 1.4 %copy.9.pos_ref = s32[6,2]{1,0:T(8,128)} copy(s32[6,2]{0,1:T(2,128)} %param.10) | data formatting | bytes 96 | tf_op args[3]
  2.6 51.9 %shard_map.86 = (f32[2,256,256]{2,1,0:T(8,128)}, f32[2,256,256]{2,1,0:T(8,128)}) custom-call(s32[6,2]{1,0:T(8,128)} %copy.9.pos_ref, s32[1]{0:T(128)S(6)} %copy.12.cnt_ref, f32[2,256,256]{2,1,0:T(8,128)} %own_hbm.1, f32[2,256,256]{2,1,0:T(8,128)} %probe_hbm.1, f32[6,256,256]{2,1,0:T(8,128)} %amp_ref.1, bf16[4,2,256,256]{3,2,1,0:T(8,128)(2,1)} %constant.4.clone.tab_hbm, ...), custom_call_target="tpu_custom_call" | custom-call | tf_op jit(solution)/shard_map/pallas_call | solution.py:412
  54.5 1.9 %copy.13 = f32[2,256,256]{2,1,0:T(8,128)} copy(f32[2,256,256]{2,1,0:T(8,128)} %get-tuple-element.4) | data formatting | bytes 1048576
  56.4 1.9 %copy.14 = f32[2,256,256]{2,1,0:T(8,128)} copy(f32[2,256,256]{2,1,0:T(8,128)} %get-tuple-element.5) | data formatting | bytes 1048576
